TPU v7x, 512 devices: a whole 4x8x8 slice. The times are simulated.
512 devices in a mesh: node: 32 (over y, z_hi, core), local: 16 (over z_lo, x).
Axes of the slice: x: 4, y: 8, z: 8 (z_hi: 2, z_lo: 4; z = z_hi * 4 + z_lo), core: 2. Of those that a mesh axis runs over, the one named last changes fastest.
Arguments:
- tokens: bfloat16 [2048, 4096], P('local', 'node'), may hold values from -6 to 6
- cotangent: bfloat16 [2048, 4096], P('local', 'node'), may hold values from -0.1875 to 0.1875
- gain: bfloat16 [1, 4096], P(None, 'node'), may hold values from 0.099609375 to 1.8984375
- up_q: bfloat16 [4096, 14336], P('local', 'node'), may hold values from -4 to 4
- up_scale: bfloat16 [32, 14336], P('local', 'node'), may hold values from 0.0078125 to 0.0390625
- down_q: bfloat16 [14336, 4096], P('node', 'local'), may hold values from -4 to 4
- down_scale: bfloat16 [14336, 32], P('node', 'local'), may hold values from 0.005004883 to 0.025024414
Outputs:
- states: bfloat16 [2048, 4096], P('local', 'node')
- grad_down: bfloat16 [14336, 4096], P('node', 'local')
All inputs are finite; a program needn't handle non-finite values.
Results may differ from a plain program's by a relative error of at most 0.035.
Values may be sent and summed in bfloat16 or wider, within the bound.
A program may use at most 64 MiB of HBM per device.

v0:
```python
import jax
import jax.numpy as jnp
from jax import lax
from jax.sharding import PartitionSpec as P

LOOPS = 2


epsilon = 1e-05


def dequant_rows(quanta, scales):
    blocks = scales.shape[0]
    widened = quanta.astype(jnp.float32).reshape(blocks, quanta.shape[0] // blocks, quanta.shape[1])
    return (
        (widened * scales.astype(jnp.float32)[:, None, :])
        .reshape(quanta.shape)
        .astype(jnp.bfloat16)
    )


def dequant_cols(quanta, scales):
    blocks = scales.shape[1]
    widened = quanta.astype(jnp.float32).reshape(quanta.shape[0], blocks, quanta.shape[1] // blocks)
    return (
        (widened * scales.astype(jnp.float32)[:, :, None])
        .reshape(quanta.shape)
        .astype(jnp.bfloat16)
    )


def normalize(values, gains):
    widened = values.astype(jnp.float32)
    meansq = jnp.mean(widened * widened, axis=-1, keepdims=True) + epsilon
    factor = lax.rsqrt(meansq)
    return ((widened * factor * gains).astype(jnp.bfloat16), factor)


def norm_backward(values, factor, gains, upstream):
    widened = values.astype(jnp.float32)
    scaled = upstream * gains
    inner = jnp.mean(scaled * widened, axis=-1, keepdims=True)
    return factor * scaled - widened * factor * factor * factor * inner


def silu_slope(pre):
    sigma = jax.nn.sigmoid(pre)
    return sigma * (1.0 + pre * (1.0 - sigma))


def per_device(tokens, cotangent, gain, up_q, up_scale, down_q, down_scale):
    values, gain_row = (
        lax.all_gather(tokens, "node", axis=1, tiled=True),
        lax.all_gather(gain, "node", axis=1, tiled=True),
    )
    gains = gain_row.astype(jnp.float32)
    up_quanta, up_scales = (
        lax.all_gather(up_q, "local", axis=0, tiled=True),
        lax.all_gather(up_scale, "local", axis=0, tiled=True),
    )
    down_quanta, down_scales = (
        lax.all_gather(down_q, "local", axis=1, tiled=True),
        lax.all_gather(down_scale, "local", axis=1, tiled=True),
    )
    up_weight = dequant_rows(up_quanta, up_scales)
    down_weight = dequant_cols(down_quanta, down_scales)
    saved = []
    for loop_index in range(LOOPS):
        normed, factor = normalize(values, gains)
        pre = jnp.dot(normed, up_weight, preferred_element_type=jnp.float32)
        hidden = jax.nn.silu(pre).astype(jnp.bfloat16)
        partial_out = jnp.dot(hidden, down_weight, preferred_element_type=jnp.float32)
        update = lax.psum(partial_out.astype(jnp.bfloat16), "node").astype(jnp.float32)
        saved.append((values, factor, pre, hidden))
        values = (values.astype(jnp.float32) + update).astype(jnp.bfloat16)
    columns_own = tokens.shape[1]
    offset = lax.axis_index("node") * columns_own
    result = lax.dynamic_slice_in_dim(values, offset, columns_own, 1)
    carried = lax.all_gather(cotangent, "node", axis=1, tiled=True)
    activations = []
    gradients = []
    for loop_index in reversed(range(LOOPS)):
        before, factor, pre, hidden = saved[loop_index]
        activations.append(hidden)
        gradients.append(carried)
        if loop_index > 0:
            slope = lax.dot_general(
                carried, down_weight, (((1,), (1,)), ((), ())), preferred_element_type=jnp.float32
            )
            pre_grad = (slope * silu_slope(pre)).astype(jnp.bfloat16)
            normed_part = lax.dot_general(
                pre_grad, up_weight, (((1,), (1,)), ((), ())), preferred_element_type=jnp.float32
            )
            normed_grad = lax.psum(normed_part.astype(jnp.bfloat16), "node").astype(jnp.float32)
            carried = (
                carried.astype(jnp.float32) + norm_backward(before, factor, gains, normed_grad)
            ).astype(jnp.bfloat16)
    acts_all = jnp.concatenate(activations, axis=0)
    grads_all = jnp.concatenate(gradients, axis=0)
    partial_grad = lax.dot_general(
        acts_all, grads_all, (((0,), (0,)), ((), ())), preferred_element_type=jnp.float32
    )
    grad_down = lax.psum_scatter(
        partial_grad.astype(jnp.bfloat16), "local", scatter_dimension=1, tiled=True
    )
    return (result, grad_down)


def solution(mesh):
    in_specs = (
        P("local", "node"),
        P("local", "node"),
        P(None, "node"),
        P("local", "node"),
        P("local", "node"),
        P("node", "local"),
        P("node", "local"),
    )
    out_specs = (P("local", "node"), P("node", "local"))
    return jax.shard_map(
        per_device, mesh=mesh, in_specs=in_specs, out_specs=out_specs, check_vma=False
    )
```

profile of v0, /device:TPU:1, one launch (start us, length us, event | category | flops | bytes accessed | tf_op | source)
XLA Modules:
  0.0 1175.4 jit_solution(14953274727109115971)
XLA Ops:
  9.4 59.2 %all_gather.22 = bf16[1,4096]{1,0:T(2,128)(2,1)S(1)} all-gather(bf16[1,128]{1,0:T(2,128)(2,1)} %param.9), channel_id=1, replica_groups=mesh['node'=32,'local'=16] {'node'}, dimensions={1}, use_global_device_ids=true | all-gather | bytes 8448 | tf_op jit(solution)/shard_map/all_gather | solution.py:54
  68.6 35.8 %all-gather = bf16[16,2,448]{2,1,0:T(2,128)(2,1)S(1)} all-gather(bf16[1,2,448]{2,1,0:T(2,128)(2,1)} %bitcast.42), channel_id=1, replica_groups=mesh['node'=32,'local'=16] {'local'}, dimensions={0}, use_global_device_ids=true | all-gather | bytes 30464 | tf_op jit(solution)/shard_map/all_gather | solution.py:59
  104.5 31.1 %all-gather.1 = bf16[16,2,448]{2,1,0:T(2,128)(2,1)S(1)} all-gather(bf16[1,2,448]{2,1,0:T(2,128)(2,1)} %bitcast.43), channel_id=1, replica_groups=mesh['node'=32,'local'=16] {'local'}, dimensions={0}, use_global_device_ids=true | all-gather | bytes 30464 | tf_op jit(solution)/shard_map/all_gather | solution.py:63
  135.8 1.5 fusion.2
  137.4 40.8 %all-gather.9.cloned.1.call-done = bf16[4096,448]{0,1:T(8,128)(2,1)} async-done(((bf16[256,448]{0,1:T(8,128)(2,1)}), bf16[4096,448]{0,1:T(8,128)(2,1)}) %all-gather.9.cloned.1.call-update) | async-done | bytes 3670032 | tf_op jit(solution)/shard_map/all_gather | solution.py:58
  178.2 2.0 mul.128
  180.2 6.3 fusion.1
  186.6 82.1 %all-gather.11.cloned.1.call-done = bf16[448,4096]{1,0:T(8,128)(2,1)} async-done(((bf16[448,256]{1,0:T(8,128)(2,1)}), bf16[448,4096]{1,0:T(8,128)(2,1)}) %all-gather.11.cloned.1.call-update) | async-done | bytes 3670032 | tf_op jit(solution)/shard_map/all_gather | solution.py:62
  268.7 2.2 mul.132
  270.9 6.8 fusion
  277.8 1.2 multiply_convert_fusion.3
  279.6 1.7 convolution_convert_fusion.3
  282.0 355.2 %all-reduce.4.cloned.1.call-done = bf16[128,4096]{1,0:T(8,128)(2,1)} async-done(((bf16[128,4096]{1,0:T(8,128)(2,1)}), bf16[128,4096]{1,0:T(8,128)(2,1)}) %all-reduce.4.cloned.1.call-update) | async-done | bytes 1048592 | tf_op jit(solution)/shard_map/psum | solution.py:73
  637.1 1.7 multiply_reduce_fusion.1
  638.8 3.4 multiply_convert_fusion.2
  642.3 1.8 convolution_convert_fusion.2
  644.1 81.6 %all-gather.13.cloned.1.call-done = bf16[128,4096]{1,0:T(8,128)(2,1)} async-done(((bf16[128,128]{1,0:T(8,128)(2,1)}), bf16[128,4096]{1,0:T(8,128)(2,1)}) %all-gather.13.cloned.1.call-update) | async-done | bytes 1048592 | tf_op jit(solution)/shard_map/all_gather | solution.py:79
  725.7 7.3 convolution_convert_fusion.1
  733.3 345.3 %all-reduce.6.cloned.1.call-done = (bf16[128,4096]{1,0:T(8,128)(2,1)}, bf16[128,4096]{1,0:T(8,128)(2,1)}) async-done(((bf16[128,4096]{1,0:T(8,128)(2,1)}, bf16[128,4096]{1,0:T(8,128)(2,1)}), (bf16[128,4096]{1,0:T(8,128)(2,1)}, bf16[128,4096]{1,0:T(8,128)(2,1)})) %all-reduce.6.cloned.1.call-update) | async-done | bytes 2097168 | tf_op jit(solution)/shard_map/psum | solution.py:73
  1078.6 1.7 multiply_reduce_fusion
  1080.3 0.8 add_convert_fusion
  1081.2 2.9 convolution_convert_fusion
  1084.4 1.4 fusion.28
  1085.8 82.8 %reduce-scatter.2.cloned.1.call-done = bf16[448,256]{1,0:T(8,128)(2,1)} async-done(((bf16[448,4096]{1,0:T(8,128)(2,1)}), bf16[448,256]{1,0:T(8,128)(2,1)}) %reduce-scatter.2.cloned.1.call-update) | async-done | bytes 229392 | tf_op jit(solution)/shard_map/reduce_scatter | solution.py:103
  (38 shorter events, 4.3 us)
Async XLA Ops:
  7.2 128.7 %all-gather.7.cloned.1.call-start = ((), (), s32[]{:S(2)}) async-start(), calls=%async_computation.1 | async-start | bytes 1081344 | tf_op jit(solution)/shard_map/all_gather | solution.py:53
  7.9 170.3 %all-gather.9.cloned.1.call-start = ((), (), s32[]{:S(2)}) async-start(), calls=%async_computation.2 | async-start | bytes 3899392 | tf_op jit(solution)/shard_map/all_gather | solution.py:58
  8.6 260.0 %all-gather.11.cloned.1.call-start = ((), (), s32[]{:S(2)}) async-start(), calls=%async_computation.3 | async-start | bytes 3899392 | tf_op jit(solution)/shard_map/all_gather | solution.py:62
  9.4 627.8 %all-reduce.4.cloned.1.call-start = ((), (), s32[]{:S(2)}) async-start(), calls=%async_computation.4 | async-start | bytes 2097152 | tf_op jit(solution)/shard_map/psum | solution.py:73
  178.2 2.0 copy-start.6
  270.9 6.9 copy-start.2
  270.9 6.9 copy-start.5
  277.7 1.9 copy-start
  281.3 444.4 %all-gather.13.cloned.1.call-start = ((), (), s32[]{:S(2)}) async-start(), calls=%async_computation.5 | async-start | bytes 1081344 | tf_op jit(solution)/shard_map/all_gather | solution.py:79
  281.9 796.7 %all-reduce.6.cloned.1.call-start = ((), (), s32[]{:S(2)}) async-start(), calls=%async_computation.7 | async-start | bytes 4194304 | tf_op jit(solution)/shard_map/psum | solution.py:73
  638.8 3.4 copy-start.1
  733.0 347.3 %copy-start.3 = (bf16[128,4096]{1,0:T(8,128)(2,1)S(1)}, bf16[128,4096]{1,0:T(8,128)(2,1)}, u32[]{:S(2)}) copy-start(bf16[128,4096]{1,0:T(8,128)(2,1)} %all-gather.13.cloned.1.call-done) | copy-start | bytes 3145732
  733.0 435.5 %reduce-scatter.2.cloned.1.call-start = ((), (), s32[]{:S(2)}) async-start(), calls=%async_computation.6 | async-start | bytes 3899392 | tf_op jit(solution)/shard_map/reduce_scatter | solution.py:103
  1078.6 1.8 copy-start.4
Sparse Core Ops, SparseCore 0:
  11.1 92.1 all-gather.6
  105.3 72.7 all-gather.8
  180.2 88.4 all-gather.10
  281.5 355.6 all-reduce.3
  640.6 85.0 all-gather.12
  733.1 345.4 all-reduce.5
  1084.3 84.2 reduce-scatter.1
where the time goes:
time: 1190 us; the launch traced here: 1180 us
  waiting for transfers between devices  990 us (83%)
  blocking collectives  126 us (11%)
  other arithmetic  20.6 us (2%)
  matrix products  18.4 us (2%)
  between operations  14.3 us (1%)
    psum x2, waiting for transfers between devices, per_device(): lax.psum(partial_out.astype(jnp.bfloat16), 'node').astype(jnp.float32)  700 us
    reduce_scatter x1, waiting for transfers between devices, per_device(): lax.psum_scatter(partial_grad.astype(jnp.bfloat16), 'local', scatter_dime...  82.8 us
    all_gather x1, waiting for transfers between devices, per_device(): lax.all_gather(down_q, 'local', axis=1, tiled=True)  82.1 us
    all_gather x1, waiting for transfers between devices, per_device(): carried = lax.all_gather(cotangent, 'node', axis=1, tiled=True)  81.6 us
    all_gather x1, blocking collectives, per_device(): lax.all_gather(gain, 'node', axis=1, tiled=True)  59.2 us
    all_gather x1, waiting for transfers between devices, per_device(): lax.all_gather(up_q, 'local', axis=0, tiled=True)  40.8 us
    all_gather x1, blocking collectives, per_device(): lax.all_gather(up_scale, 'local', axis=0, tiled=True)  35.8 us
    all_gather x1, blocking collectives, per_device(): lax.all_gather(down_scale, 'local', axis=1, tiled=True)  31.1 us
  transfers between devices with their start and end apart: 7, of which 6 were waited for; matrix products, arithmetic and copies ran while one was open for 2% of the time, Pallas kernels for 0%

commit v1 on v0

v1 whole, which is shorter than its diff:
```python
import jax
import jax.numpy as jnp
from jax import lax
from jax.experimental import pallas as pl
from jax.experimental.pallas import tpu as pltpu
from jax.sharding import PartitionSpec as P

MESH = pl.DeviceIdType.MESH
BF = jnp.bfloat16
F32 = jnp.float32
EPS = 1e-05
NT = (((1,), (1,)), ((), ()))
NN = (((1,), (0,)), ((), ()))


def dequant_rows(quanta, scales):
    blocks = scales.shape[0]
    widened = quanta.astype(F32).reshape(blocks, quanta.shape[0] // blocks, quanta.shape[1])
    return (widened * scales.astype(F32)[:, None, :]).reshape(quanta.shape).astype(BF)


def dequant_cols(quanta, scales):
    blocks = scales.shape[1]
    widened = quanta.astype(F32).reshape(quanta.shape[0], blocks, quanta.shape[1] // blocks)
    return (widened * scales.astype(F32)[:, :, None]).reshape(quanta.shape).astype(BF)


def peer(j):
    far = j // 2 + 1
    return far + (j % 2) * (8 - 2 * far)


def flip(a, i):
    return ((a // 2 + i // 2) % 2) * 2 + (a % 2 + i % 2) % 2


class Sems:
    def __init__(self):
        self.used = 0

    def take(self, count):
        base = self.used
        self.used += count
        return base


N_SEMS = 276


def kernel(
    up_in, dn_in, tok_in, cot_in, states_out, grad_out,
    up, dn, x0, x1, cot, cott, g1t, nb, h1t, h2t, hid, hf, pre, slope, gacc, fac, gp, tot,
    po1, ps1, r11, r21, r31, t31,
    pog, psg, r1g, r2g, r3g, t3g,
    po2, ps2, r12, r22, r32, t32,
    ss, rs,
):
    n = lax.axis_index("node")
    l = lax.axis_index("local")
    y, zh, c = n // 4, (n // 2) % 2, n % 2
    zl, x = l // 4, l % 4
    sems = Sems()

    def node_of(y_, zh_, c_):
        return (y_ * 2 + zh_) * 2 + c_

    sib = (node_of(y, zh, 1 - c), l)
    zhp = (node_of(y, 1 - zh, c), l)
    own_m = node_of(y, 1 - zh, c)

    def ydev(k):
        return (node_of((y + k) % 8, zh, c), l)

    def xdev(d):
        return (n, zl * 4 + (x + d + 4) % 4)

    def zdev(i):
        return (n, flip(zl, i) * 4 + x)

    part_n, part_l = l * 2 + c, n // 2
    moved = part_l != l
    part = (part_n, part_l)

    def rc(src, dst, sem, dev):
        return pltpu.make_async_remote_copy(
            src_ref=src, dst_ref=dst, send_sem=ss.at[sem], recv_sem=rs.at[sem],
            device_id=dev, device_id_type=MESH,
        )

    def loop(count, body):
        def step(j, carry):
            body(j)
            return carry
        lax.fori_loop(0, count, step, 0)

    class NodeGather:
        def __init__(self, buf):
            self.buf, self.base = buf, sems.take(31)

        def copy(self, slot, sem, dev):
            return rc(self.buf.at[slot], self.buf.at[slot], self.base + sem, dev)

        def own_y(self, j):
            return self.copy(n, 2 + j, ydev(peer(j)))

        def other_y(self, j):
            return self.copy(own_m, 9 + j, ydev(peer(j)))

        def from_y(self, j, zh_):
            return node_of((y - peer(j) + 8) % 8, zh_, c)

        def fwd_own(self, j):
            return self.copy(self.from_y(j, zh), 17 + j, sib)

        def fwd_other(self, j):
            return self.copy(self.from_y(j, 1 - zh), 24 + j, sib)

        def start(self):
            self.copy(n, 1, zhp).start()
            self.copy(n, 0, sib).start()
            loop(7, lambda j: self.own_y(j).start())

        def mid(self):
            self.copy(n, 1, zhp).wait_recv()
            loop(7, lambda j: self.other_y(j).start())
            self.copy(own_m, 16, sib).start()

        def forward(self):
            def first(j):
                self.own_y(j).wait_recv()
                self.fwd_own(j).start()

            def second(j):
                self.other_y(j).wait_recv()
                self.fwd_other(j).start()

            loop(7, first)
            loop(7, second)

        def end(self):
            self.copy(n, 0, sib).wait_recv()
            self.copy(own_m, 16, sib).wait_recv()
            loop(7, lambda j: self.fwd_own(j).wait_recv())
            loop(7, lambda j: self.fwd_other(j).wait_recv())

        def drain(self):
            self.copy(n, 0, sib).wait_send()
            self.copy(n, 1, zhp).wait_send()
            self.copy(own_m, 16, sib).wait_send()

            def sent(j):
                self.own_y(j).wait_send()
                self.other_y(j).wait_send()
                self.fwd_own(j).wait_send()
                self.fwd_other(j).wait_send()

            loop(7, sent)

    class LocalGather:
        def __init__(self, buf):
            self.buf, self.base = buf, sems.take(19)
            self.half = buf.shape[1] // 2

        def slot(self, i, d):
            return flip(zl, i) * 4 + (x + d + 4) % 4

        def zc(self, i):
            return rc(self.buf.at[l], self.buf.at[l], self.base + i - 1, zdev(i))

        def fc(self, i, d):
            s = self.slot(i, 0)
            return rc(self.buf.at[s], self.buf.at[s], self.base + 3 + 4 * i + (d < 0), xdev(d))

        def relc(self, i, d):
            s = self.slot(i, -d)
            rows = pl.ds(0 if d > 0 else self.half, self.half)
            ref = self.buf.at[s, rows]
            return rc(ref, ref, self.base + 5 + 4 * i + (d < 0), xdev(d))

        def z(self, i):
            self.zc(i).start()

        def wait_z(self, i):
            self.zc(i).wait_recv()

        def full(self, i):
            self.fc(i, 1).start()
            self.fc(i, -1).start()

        def relay(self, i):
            self.fc(i, 1).wait_recv()
            self.relc(i, 1).start()
            self.fc(i, -1).wait_recv()
            self.relc(i, -1).start()

        def done(self, i):
            self.relc(i, 1).wait_recv()
            self.relc(i, -1).wait_recv()

        def drain(self):
            for i in range(1, 4):
                self.zc(i).wait_send()
            for i in range(4):
                for d in (1, -1):
                    self.fc(i, d).wait_send()
                    self.relc(i, d).wait_send()

    class NodeReduce:
        def __init__(self, po, ps, r1, r2, r3, t3):
            self.po, self.ps, self.r1, self.r2, self.r3, self.t3 = po, ps, r1, r2, r3, t3
            self.base = sems.take(13)

        def sib_copy(self, i):
            rows = pl.ds(flip(zl, i) * 4, 4)
            return rc(self.ps.at[rows], self.r1.at[rows], self.base + i, sib)

        def y_copy(self, j):
            to = (y + peer(j)) % 8
            return rc(self.po.at[pl.ds(to * 2, 2)], self.r2.at[y], self.base + 4 + j, ydev(peer(j)))

        def zh_copy(self):
            return rc(self.t3, self.r3, self.base + 11, zhp)

        def send(self, i):
            self.sib_copy(i).start()

        def combine(self, i):
            self.sib_copy(i).wait_recv()
            first = flip(zl, i) * 4

            def add(q):
                s = first + q
                self.po[s] = (self.po[s].astype(F32) + self.r1[s].astype(F32)).astype(BF)

            loop(4, add)

        def spread(self):
            loop(7, lambda j: self.y_copy(j).start())

        def total(self, zh_):
            def add(j, acc):
                return acc + self.r2[(y - peer(j) + 8) % 8, zh_].astype(F32)

            return lax.fori_loop(0, 7, add, self.po[y * 2 + zh_].astype(F32))

        def cross(self):
            loop(7, lambda j: self.y_copy(j).wait_recv())
            self.t3[...] = self.total(1 - zh).astype(BF)
            self.zh_copy().start()

        def finish(self):
            mine = self.total(zh)
            self.zh_copy().wait_recv()
            return mine + self.r3[...].astype(F32)

        def drain(self):
            for i in range(4):
                self.sib_copy(i).wait_send()
            loop(7, lambda j: self.y_copy(j).wait_send())
            self.zh_copy().wait_send()

    perm_base = sems.take(2)

    def perm_copy(src, dst, which):
        return rc(src, dst.at[part_n], perm_base + which, part)

    def perm_start(src, dst, which):
        @pl.when(moved)
        def _():
            perm_copy(src, dst, which).start()

        @pl.when(jnp.logical_not(moved))
        def _():
            dst[n] = src[...]

    def perm_wait(src, dst, which):
        @pl.when(moved)
        def _():
            perm_copy(src, dst, which).wait_recv()

    def perm_drain(src, dst, which):
        @pl.when(moved)
        def _():
            perm_copy(src, dst, which).wait_send()

    def rms_factor(buf):
        def add(j, acc):
            v = buf[j, 0:128, :].astype(F32)
            return acc + v * v

        sums = lax.fori_loop(0, 32, add, jnp.zeros((128, 128), F32))
        factor = lax.rsqrt(jnp.sum(sums, axis=1, keepdims=True) / 4096.0 + EPS)
        fac[...] = jnp.broadcast_to(factor, (128, 128))

    def gain_row(j):
        return x0[j, 128:144, :].astype(F32)[0:1, :]

    def normalize(buf):
        rms_factor(buf)

        def one(q):
            for h in range(2):
                j = q * 2 + h
                v = buf[j, 0:128, :].astype(F32) * fac[...] * gain_row(j)
                nb[q, :, h * 128:(h + 1) * 128] = v.astype(BF)

        loop(16, one)

    def up_chunk(q):
        pre[...] += lax.dot_general(nb[q], up[q], NT, preferred_element_type=F32)

    def pre_item(i):
        loop(4, lambda q: up_chunk(flip(zl, i) * 4 + q))

    def slope_chunk(q):
        rows = jnp.concatenate([cot[q * 2], cot[q * 2 + 1]], axis=1)
        slope[...] += lax.dot_general(rows, dn[q], NT, preferred_element_type=F32)

    def activate(transposed):
        v = pre[...]
        h = v * jax.nn.sigmoid(v)
        hid[...] = h.astype(BF)
        hf[:, 0:448] = h
        for b in range(4):
            rows = 128 if b < 3 else 64
            block = hf[:, b * 128:(b + 1) * 128].T
            transposed[l, b * 128:b * 128 + rows, :] = block[0:rows, :].astype(BF)

    def out_chunk(left, weight, q, red):
        res = lax.dot_general(left, weight[q], NN, preferred_element_type=F32).astype(BF)
        low, high = res[:, 0:128], res[:, 128:256]
        even = c == 0
        red.po[q, 0:128, :] = jnp.where(even, low, high)
        red.ps[q, 0:128, :] = jnp.where(even, high, low)

    def out_item(left, weight, i, red):
        loop(4, lambda q: out_chunk(left[...], weight, flip(zl, i) * 4 + q, red))
        red.send(i)

    ag_x0, ag_cot, ag_cott, ag_x1, ag_g1 = (NodeGather(b) for b in (x0, cot, cott, x1, g1t))
    lg_up, lg_dn, lg_h1, lg_h2 = (LocalGather(b) for b in (up, dn, h1t, h2t))
    rs_1 = NodeReduce(po1, ps1, r11, r21, r31, t31)
    rs_g = NodeReduce(pog, psg, r1g, r2g, r3g, t3g)
    rs_2 = NodeReduce(po2, ps2, r12, r22, r32, t32)
    assert sems.used <= N_SEMS, sems.used

    barrier = pltpu.get_barrier_semaphore()

    def greet(dev):
        pl.semaphore_signal(barrier, inc=1, device_id=dev, device_id_type=MESH)

    @pl.when(moved)
    def _():
        greet(part)

    greet(zhp)
    loop(7, lambda j: greet(ydev(peer(j))))
    for i in range(1, 4):
        greet(zdev(i))
    greet(xdev(1))
    greet(xdev(-1))
    greet(sib)

    up[l] = up_in[...]
    dn[l] = dn_in[...]
    x0[n] = tok_in[...]
    cot[n] = cot_in[...]
    hf[...] = jnp.zeros_like(hf)
    pre[...] = jnp.zeros_like(pre)
    slope[...] = jnp.zeros_like(slope)

    @pl.when(moved)
    def _():
        pl.semaphore_wait(barrier, 15)

    @pl.when(jnp.logical_not(moved))
    def _():
        pl.semaphore_wait(barrier, 14)

    ag_x0.start()
    lg_up.z(1)
    lg_up.full(0)
    lg_up.z(2)
    perm_start(cot_in, cott, 0)
    ag_x0.mid()
    lg_up.relay(0)
    lg_up.wait_z(1)
    lg_up.z(3)
    lg_up.full(1)
    lg_up.wait_z(2)
    lg_up.full(2)
    ag_x0.forward()
    ag_cot.start()
    ag_x0.end()
    normalize(x0)
    lg_up.relay(1)
    lg_up.done(0)
    pre_item(0)
    lg_up.wait_z(3)
    lg_up.full(3)
    lg_dn.z(1)
    lg_dn.z(2)
    ag_cot.mid()
    lg_up.relay(2)
    lg_up.done(1)
    pre_item(1)
    lg_up.relay(3)
    lg_dn.full(0)
    lg_up.done(2)
    pre_item(2)
    lg_dn.wait_z(1)
    lg_dn.z(3)
    lg_dn.full(1)
    lg_up.done(3)
    pre_item(3)
    activate(h1t)
    lg_dn.relay(0)
    lg_dn.wait_z(2)
    lg_dn.full(2)
    ag_cot.forward()
    ag_cot.end()
    perm_wait(cot_in, cott, 0)
    ag_cott.start()
    lg_dn.relay(1)
    lg_dn.done(0)
    out_item(hid, dn, 0, rs_1)
    lg_dn.wait_z(3)
    lg_dn.full(3)
    ag_cott.mid()
    lg_dn.relay(2)
    lg_dn.done(1)
    out_item(hid, dn, 1, rs_1)
    rs_1.combine(0)
    lg_dn.relay(3)
    lg_dn.done(2)
    out_item(hid, dn, 2, rs_1)
    rs_1.combine(1)
    ag_cott.forward()
    lg_dn.done(3)
    out_item(hid, dn, 3, rs_1)
    rs_1.combine(2)
    rs_1.combine(3)
    rs_1.spread()
    for i in range(1, 4):
        lg_h1.z(i)
    loop(16, slope_chunk)
    rs_1.cross()
    lg_h1.full(0)
    for i in range(1, 4):
        lg_h1.wait_z(i)
        lg_h1.full(i)
    ag_cott.end()
    x1[n] = (x0[n, 0:128, :].astype(F32) + rs_1.finish()).astype(BF)

    ag_x1.start()
    pre[...] = jnp.zeros_like(pre)
    ag_x1.mid()
    for i in range(4):
        lg_h1.relay(i)
    ag_x1.forward()
    ag_x1.end()
    normalize(x1)
    loop(16, up_chunk)
    activate(h2t)

    v = pre[...]
    sig = jax.nn.sigmoid(v)
    grad_pre = (slope[...] * (sig * (1.0 + v * (1.0 - sig)))).astype(BF)
    pulled = jnp.sum(grad_pre.astype(F32) * v, axis=1, keepdims=True)
    pulled = jnp.broadcast_to(pulled, (128, 128)).T[0:16, :].astype(BF)

    def put(j):
        pog[j, 128:144, :] = pulled
        psg[j, 128:144, :] = pulled

    loop(16, put)
    for i in range(4):
        loop(4, lambda q: out_chunk(grad_pre, up, flip(zl, i) * 4 + q, rs_g))
        rs_g.send(i)
    for i in range(4):
        rs_g.combine(i)
    rs_g.spread()
    for i in range(1, 4):
        lg_h2.z(i)
    lg_h2.full(0)
    for i in range(4):
        out_item(hid, dn, i, rs_2)
    for i in range(4):
        rs_2.combine(i)
    rs_g.cross()
    rs_2.spread()
    for i in range(1, 4):
        lg_h2.wait_z(i)
        lg_h2.full(i)
    tot[...] = rs_g.finish()
    inner = jnp.broadcast_to(tot[128:129, :], (128, 128)).T / 4096.0
    x1_own = x1[n].astype(F32)
    scaled = tot[0:128, :] * gain_row(n)
    factor = fac[...]
    gp[...] = (cot[n].astype(F32) + factor * scaled - x1_own * factor * factor * inner).astype(BF)
    perm_start(gp, g1t, 1)
    for i in range(4):
        lg_h2.relay(i)
        lg_h1.done(i)
    perm_wait(gp, g1t, 1)
    ag_g1.start()
    rs_2.cross()
    gacc[...] = jnp.zeros_like(gacc)
    for i in range(4):
        lg_h2.done(i)

    def grad_chunk(hidden, grads):
        def one(q):
            right = jnp.concatenate([grads[q * 2], grads[q * 2 + 1]], axis=1)
            gacc[...] += lax.dot_general(hidden[q], right, NN, preferred_element_type=F32)
        return one

    ag_g1.mid()
    loop(16, grad_chunk(h2t, cott))
    states_out[...] = (x1_own + rs_2.finish()).astype(BF)
    ag_g1.forward()
    ag_g1.end()
    loop(16, grad_chunk(h1t, g1t))
    grad_out[...] = gacc[...].astype(BF)

    for g in (ag_x0, ag_cot, ag_cott, ag_x1, ag_g1, lg_up, lg_dn, lg_h1, lg_h2, rs_1, rs_g, rs_2):
        g.drain()
    perm_drain(cot_in, cott, 0)
    perm_drain(gp, g1t, 1)


def per_device(tokens, cotangent, gain, up_q, up_scale, down_q, down_scale):
    up = dequant_rows(up_q, up_scale).T
    down = dequant_cols(down_q, down_scale)
    tok = jnp.concatenate([tokens, jnp.broadcast_to(gain, (16, 128))], axis=0)
    vmem = pl.BlockSpec(memory_space=pltpu.VMEM)

    def reduce_scratch(rows):
        wide = pltpu.VMEM((16, rows, 128), BF)
        one = pltpu.VMEM((rows, 128), BF)
        return [wide, wide, wide, pltpu.VMEM((8, 2, rows, 128), BF), one, one]

    full = pltpu.VMEM((16, 448, 256), BF)
    act = pltpu.VMEM((32, 128, 128), BF)
    hidden_all = pltpu.VMEM((16, 448, 128), BF)
    scratch = [
        full, full, pltpu.VMEM((32, 144, 128), BF), act, act, act, act,
        pltpu.VMEM((16, 128, 256), BF), hidden_all, hidden_all,
        pltpu.VMEM((128, 448), BF), pltpu.VMEM((128, 512), F32),
        pltpu.VMEM((128, 448), F32), pltpu.VMEM((128, 448), F32),
        pltpu.VMEM((448, 256), F32), pltpu.VMEM((128, 128), F32),
        pltpu.VMEM((128, 128), BF), pltpu.VMEM((144, 128), F32),
    ]
    scratch += reduce_scratch(128) + reduce_scratch(144) + reduce_scratch(128)
    scratch += [pltpu.SemaphoreType.DMA((N_SEMS,)), pltpu.SemaphoreType.DMA((N_SEMS,))]
    return pl.pallas_call(
        kernel,
        out_shape=(
            jax.ShapeDtypeStruct((128, 128), BF),
            jax.ShapeDtypeStruct((448, 256), BF),
        ),
        in_specs=[vmem] * 4,
        out_specs=(vmem, vmem),
        scratch_shapes=scratch,
        compiler_params=pltpu.CompilerParams(
            collective_id=0, has_side_effects=True, vmem_limit_bytes=48 << 20
        ),
        name="looped_block",
    )(up, down, tok, cotangent)


def solution(mesh):
    in_specs = (
        P("local", "node"),
        P("local", "node"),
        P(None, "node"),
        P("local", "node"),
        P("local", "node"),
        P("node", "local"),
        P("node", "local"),
    )
    out_specs = (P("local", "node"), P("node", "local"))
    return jax.shard_map(
        per_device, mesh=mesh, in_specs=in_specs, out_specs=out_specs, check_vma=False
    )
```

time: 1190 us -> 197 us (0.17)
  the two profiles are of different devices: /device:TPU:1 before, /device:TPU:27 now
where the time goes in v1:
time: 197 us
  Pallas kernels  190 us (96%)
  local copies, waits for them, and re-layouts  6.24 us (3%)
    pallas_call x1, Pallas kernels, per_device(): pl.pallas_call(kernel, out_shape=(jax.ShapeDtypeStruct((128, 128), BF), j...  190 us
    unnamed x14, local copies, waits for them, and re-layouts  4.18 us

profile of v1, /device:TPU:27, one launch (start us, length us, event | category | flops | bytes accessed | tf_op | source)
XLA Modules:
  0.0 196.7 jit_solution(14831590246729304304)
XLA Ops:
  0.6 0.8 copy.10
  1.5 0.0 copy-start.1
  1.5 0.5 mul.25
  2.0 0.4 copy-done.1
  2.4 0.0 copy-start.4
  2.4 0.1 fusion.dn_in
  2.5 0.6 copy-done.4
  3.1 0.2 copy.9
  3.2 0.0 copy-start.2
  3.3 0.5 mul.22
  3.8 0.4 copy-done.2
  4.2 0.0 copy-start.3
  4.2 0.1 fusion.2.up_in
  4.2 0.0 copy-start.5
  4.3 0.6 copy-done.5
  4.9 0.0 copy-done.3
  5.0 0.0 copy-start
  5.0 0.8 copy-done
  5.7 189.7 %looped_block.1 = (bf16[128,128]{1,0:T(8,128)(2,1)S(1)}, bf16[448,256]{1,0:T(8,128)(2,1)S(1)}) custom-call(bf16[448,256]{1,0:T(8,128)(2,1)S(1)} %fusion.2.up_in, bf16[448,256]{1,0:T(8,128)(2,1)S(1)} %fusion.dn_in, bf16[144,128]{1,0:T(8,128)(2,1)S(1)} %pad_maximum_fusion.tok_in, bf16[128,128]{1,0:T(8,128)(2,1)S(1)} %copy-done), custom_call_target="tpu_custom_call" | custom-call | tf_op jit(solution)/shard_map/looped_block/pallas_call | solution.py:556
  195.4 0.6 copy.19
  196.1 0.7 copy.20
  (2 shorter events, 0.0 us)
Async XLA Ops:
  1.5 0.9 copy-start.1
  2.4 0.7 copy-start.4
  3.2 0.9 copy-start.2
  4.2 0.8 copy-start.3
  4.2 0.7 copy-start.5
  5.0 0.8 copy-start

commit v2 on v1

v2 whole, which is shorter than its diff:
```python
import jax
import jax.numpy as jnp
from jax import lax
from jax.experimental import pallas as pl
from jax.experimental.pallas import tpu as pltpu
from jax.sharding import PartitionSpec as P

MESH = pl.DeviceIdType.MESH
BF = jnp.bfloat16
F32 = jnp.float32
EPS = 1e-05
NT = (((1,), (1,)), ((), ()))
NN = (((1,), (0,)), ((), ()))


def peer(j):
    far = j // 2 + 1
    return far + (j % 2) * (8 - 2 * far)


def flip(a, i):
    return ((a // 2 + i // 2) % 2) * 2 + (a % 2 + i % 2) % 2


class Sems:
    def __init__(self):
        self.used = 0

    def take(self, count):
        base = self.used
        self.used += count
        return base


N_SEND = 24
N_RECV = 152


def kernel(
    tok_in, cot_in, gain_in, up_q, up_s, dn_q, dn_s, states_out, grad_out,
    up, dn, x0, x1, cot, cott, g1t, nb, h1t, h2t, hid, hf, pre, slope, gacc, fac, gp, tot,
    po1, ps1, r11, r21, r31, t31,
    pog, psg, r1g, r2g, r3g, t3g,
    po2, ps2, r12, r22, r32, t32,
    ss, rs,
):
    n = lax.axis_index("node")
    l = lax.axis_index("local")
    y, zh, c = n // 4, (n // 2) % 2, n % 2
    zl, x = l // 4, l % 4
    sends, recvs = Sems(), Sems()

    def node_of(y_, zh_, c_):
        return (y_ * 2 + zh_) * 2 + c_

    sib = (node_of(y, zh, 1 - c), l)
    zhp = (node_of(y, 1 - zh, c), l)
    own_m = node_of(y, 1 - zh, c)

    def ydev(k):
        return (node_of((y + k) % 8, zh, c), l)

    def xdev(d):
        return (n, zl * 4 + (x + d + 4) % 4)

    def zdev(i):
        return (n, flip(zl, i) * 4 + x)

    moved = n // 2 != l

    def rc(src, dst, send, recv, dev):
        return pltpu.make_async_remote_copy(
            src_ref=src, dst_ref=dst, send_sem=ss.at[send], recv_sem=rs.at[recv],
            device_id=dev, device_id_type=MESH,
        )

    def loop(count, body, first=0, unroll=1):
        if count - first == 1:
            body(first)
            return

        def step(j, carry):
            body(j)
            return carry

        lax.fori_loop(first, count, step, 0, unroll=unroll)

    pending = {}
    departures = []

    def go(key, count, copy):
        assert key not in pending
        pending[key] = count, copy
        loop(count, lambda j: copy(j).start())

    def got(key):
        count, copy = pending.pop(key)
        loop(count, lambda j: copy(j).wait_recv())

    def departing(view):
        sem = sends.take(1)
        departures.append((view, sem))
        return sem

    def drain():
        assert not pending
        for view, sem in departures:
            rc(view, view, sem, 0, sib).wait_send()

    class NodeGather:
        def __init__(self, buf, base):
            self.buf, self.base = buf, base
            self.left = departing(buf.at[pl.ds(0, 31)])

        def copy(self, slot, sem, dev):
            return rc(self.buf.at[slot], self.buf.at[slot], self.left, self.base + sem, dev)

        def from_y(self, j, zh_):
            return node_of((y - peer(j) + 8) % 8, zh_, c)

        def start(self):
            go((self, "zh"), 1, lambda j: self.copy(n, 1, zhp))
            go((self, "own"), 7, lambda j: self.copy(n, 2 + j, ydev(peer(j))))
            go((self, "sib"), 1, lambda j: self.copy(n, 0, sib))

        def mid(self):
            got((self, "zh"))
            go((self, "other"), 7, lambda j: self.copy(own_m, 9 + j, ydev(peer(j))))
            go((self, "sib_zh"), 1, lambda j: self.copy(own_m, 16, sib))

        def pass_on(self, key, zh_, sem, use):
            count, came = pending.pop((self, key))

            def copy(j):
                return self.copy(self.from_y(j, zh_), sem + j, sib)

            def move(j):
                came(j).wait_recv()
                copy(j).start()

            def finish(j):
                copy(j).wait_recv()
                use(((y - peer(j) + 8) % 8) * 2 + zh_)

            def both(j):
                move(j)
                finish(j - 1)

            move(0)
            loop(count, both, first=1)
            finish(count - 1)

        def end(self, use=lambda q: None):
            got((self, "sib"))
            use(y * 2 + zh)
            got((self, "sib_zh"))
            use(y * 2 + 1 - zh)
            self.pass_on("own", zh, 17, use)
            self.pass_on("other", 1 - zh, 24, use)

    class SeededGather:
        def __init__(self, buf, base):
            self.buf, self.base, self.perm = buf, base, recvs.take(4)
            self.left = departing(buf.at[pl.ds(0, 28)])
            self.perm_left = sends.take(4)

        def seed(self, k):
            return node_of((y + 4 * (k // 2)) % 8, (zh + k % 2) % 2, c)

        def scatter_copy(self, src, k):
            to = node_of((l // 2 + 4 * (k // 2)) % 8, (l % 2 + k % 2) % 2, c)
            return rc(src, self.buf.at[l * 2 + c], self.perm_left + k, self.perm + k, (to, n // 2))

        def scatter(self, src):
            @pl.when(moved)
            def _():
                self.scatter_copy(src, 0).start()

            @pl.when(jnp.logical_not(moved))
            def _():
                self.buf[l * 2 + c] = src[...]

            for k in range(1, 4):
                self.scatter_copy(src, k).start()

        def seeded(self, src):
            @pl.when(moved)
            def _():
                self.scatter_copy(src, 0).wait_recv()

            for k in range(1, 4):
                self.scatter_copy(src, k).wait_recv()

        def scattered(self, src):
            @pl.when(moved)
            def _():
                self.scatter_copy(src, 0).wait_send()

            for k in range(1, 4):
                self.scatter_copy(src, k).wait_send()

        def copy(self, slot, sem, dev):
            return rc(self.buf.at[slot], self.buf.at[slot], self.left, self.base + sem, dev)

        def step(self, r, k):
            return (1, 7)[r] if r < 2 else 2 + 4 * (k % 2)

        def spread(self):
            for r in range(3):
                loop(4, lambda k: self.copy(self.seed(k), r * 4 + k, ydev(self.step(r, k))).start())
            loop(4, lambda k: self.copy(self.seed(k), 12 + k, sib).start())

        def arrival(self, r, k):
            from_y = (y - self.step(r, k) + 8) % 8
            return node_of((from_y + 4 * (k // 2)) % 8, (zh + k % 2) % 2, c)

        def end(self, use):
            def move(r, k):
                slot = self.arrival(r, k)
                self.copy(slot, r * 4 + k, sib).wait_recv()
                self.copy(slot, 16 + r * 4 + k, sib).start()

            def finish(r, k):
                slot = self.arrival(r, k)
                self.copy(slot, 16 + r * 4 + k, sib).wait_recv()
                use(slot // 2)

            def seeds(k):
                self.copy(self.seed(k), 12 + k, sib).wait_recv()
                use(self.seed(k) // 2)

            loop(4, seeds)
            for r in range(3):
                loop(4, lambda k: move(r, k))
                if r > 0:
                    loop(4, lambda k: finish(r - 1, k))
            loop(4, lambda k: finish(2, k))

    class LocalGather:
        def __init__(self, buf, base):
            self.buf, self.base = buf, base
            self.half = buf.shape[1] // 2
            self.left = departing(buf.at[pl.ds(0, 15)])

        def slot(self, i, d):
            return flip(zl, i) * 4 + (x + d + 4) % 4

        def z(self, i):
            go((self, "z", i), 1, lambda j: rc(self.buf.at[l], self.buf.at[l], self.left, self.base + i - 1, zdev(i)))

        def wait_z(self, i):
            got((self, "z", i))

        def full(self, i):
            s = self.buf.at[self.slot(i, 0)]
            for d in (1, -1):
                go((self, "x", i, d), 1, lambda j, d=d: rc(s, s, self.left, self.base + 3 + 2 * i + (d < 0), xdev(d)))

        def relay(self, i):
            for d in (1, -1):
                ref = self.buf.at[self.slot(i, -d), pl.ds(0 if d > 0 else self.half, self.half)]
                got((self, "x", i, d))
                rc(ref, ref, self.left, self.base + 11 + i, xdev(d)).start()

        def done(self, i):
            s = self.buf.at[self.slot(i, 2)]
            rc(s, s, self.left, self.base + 11 + i, xdev(1)).wait_recv()

    class NodeReduce:
        def __init__(self, po, ps, r1, r2, r3, t3):
            self.po, self.ps, self.r1, self.r2, self.r3, self.t3 = po, ps, r1, r2, r3, t3
            self.base = recvs.take(7)
            self.sib_left = departing(ps)
            self.left = departing(po.at[pl.ds(0, 15)])

        def send(self, i):
            rows = pl.ds(flip(zl, i) * 4, 4)
            go((self, "sib", i), 1, lambda j: rc(self.ps.at[rows], self.r1.at[rows], self.sib_left, self.base + i, sib))

        def combine(self, i):
            got((self, "sib", i))
            first = flip(zl, i) * 4

            def add(q):
                s = first + q
                self.po[s] = (self.po[s].astype(F32) + self.r1[s].astype(F32)).astype(BF)

            loop(4, add, unroll=True)

        def spread(self, kind, i):
            for q in range(2):
                to = flip(zl, i) * 2 + q
                src = self.po.at[to * 2 + (1 - zh if kind == 0 else zh)]

                @pl.when(to != y)
                def _():
                    rc(src, self.r2.at[kind, y], self.left, self.base + 4 + kind, (node_of(to, zh, c), l)).start()

        def arrive(self, kind):
            view = self.r2.at[kind, pl.ds(0, 7)]
            rc(view, view, self.left, self.base + 4 + kind, sib).wait_recv()

        def total(self, kind):
            def add(j, acc):
                return acc + self.r2[kind, (y - peer(j) + 8) % 8].astype(F32)

            return lax.fori_loop(0, 7, add, self.po[y * 2 + (1 - zh if kind == 0 else zh)].astype(F32), unroll=True)

        def cross(self):
            self.arrive(0)
            self.t3[...] = self.total(0).astype(BF)
            go((self, "zh"), 1, lambda j: rc(self.t3, self.r3, self.left, self.base + 6, zhp))

        def finish(self):
            mine = self.total(1)
            got((self, "zh"))
            return mine + self.r3[...].astype(F32)

    def factor_of(sums):
        return lax.rsqrt(jnp.sum(sums, axis=1, keepdims=True) / 4096.0 + EPS)

    def rms_factor(buf):
        def add(j, acc):
            v = buf[j, 0:128, :].astype(F32)
            return acc + v * v

        sums = lax.fori_loop(0, 32, add, jnp.zeros((128, 128), F32), unroll=4)
        fac[...] = jnp.broadcast_to(factor_of(sums), (128, 128))

    def gain_row(j):
        return x0[j, 128:144, :].astype(F32)[0:1, :]

    def normalize(buf):
        rms_factor(buf)

        def one(q):
            for h in range(2):
                j = q * 2 + h
                v = buf[j, 0:128, :].astype(F32) * fac[...] * gain_row(j)
                nb[q, :, h * 128:(h + 1) * 128] = v.astype(BF)

        loop(16, one, unroll=4)

    def up_chunk(q):
        pre[...] += lax.dot_general(nb[q], up[q], NT, preferred_element_type=F32)

    def pre_item(i):
        loop(4, lambda q: up_chunk(flip(zl, i) * 4 + q), unroll=True)

    def raw_chunk(q):
        halves = []
        for h in range(2):
            v = x1[q * 2 + h].astype(F32)
            fac[...] += v * v
            halves.append((v * gain_row(q * 2 + h)).astype(BF))
        pre[...] += lax.dot_general(jnp.concatenate(halves, axis=1), up[q], NT, preferred_element_type=F32)

    def slope_chunk(q):
        rows = jnp.concatenate([cot[q * 2], cot[q * 2 + 1]], axis=1)
        slope[...] += lax.dot_general(rows, dn[q], NT, preferred_element_type=F32)

    def activate(transposed):
        v = pre[...]
        h = v * jax.nn.sigmoid(v)
        hid[...] = h.astype(BF)
        hf[:, 0:448] = h
        for b in range(4):
            rows = 128 if b < 3 else 64
            block = hf[:, b * 128:(b + 1) * 128].T
            transposed[l, b * 128:b * 128 + rows, :] = block[0:rows, :].astype(BF)

    def out_chunk(left, weight, q, red):
        res = lax.dot_general(left, weight[q], NN, preferred_element_type=F32).astype(BF)
        low, high = res[:, 0:128], res[:, 128:256]
        even = c == 0
        red.po[q, 0:128, :] = jnp.where(even, low, high)
        red.ps[q, 0:128, :] = jnp.where(even, high, low)

    def out_item(left, weight, i, red):
        loop(4, lambda q: out_chunk(left[...], weight, flip(zl, i) * 4 + q, red), unroll=True)
        red.send(i)

    ag_a, ag_b, sg_a, lg_a, lg_b = (recvs.take(k) for k in (31, 31, 28, 15, 15))
    ag_x0, ag_cot, ag_x1 = NodeGather(x0, ag_a), NodeGather(cot, ag_b), NodeGather(x1, ag_a)
    sg_cot, sg_g1 = SeededGather(cott, sg_a), SeededGather(g1t, sg_a)
    lg_up, lg_dn = LocalGather(up, lg_a), LocalGather(dn, lg_b)
    lg_h1, lg_h2 = LocalGather(h1t, lg_a), LocalGather(h2t, lg_b)
    rs_1 = NodeReduce(po1, ps1, r11, r21, r31, t31)
    rs_g = NodeReduce(pog, psg, r1g, r2g, r3g, t3g)
    rs_2 = NodeReduce(po2, ps2, r12, r22, r32, t32)
    assert sends.used <= N_SEND and recvs.used <= N_RECV, (sends.used, recvs.used)

    barrier = pltpu.get_barrier_semaphore()

    def greet(dev):
        pl.semaphore_signal(barrier, inc=1, device_id=dev, device_id_type=MESH)

    for k in range(4):
        source = node_of((y + 4 * (k // 2)) % 8, (zh + k % 2) % 2, c) // 2
        if k == 0:
            @pl.when(moved)
            def _():
                greet((l * 2 + c, source))
        else:
            greet((l * 2 + c, source))

    greet(zhp)
    loop(7, lambda j: greet(ydev(peer(j))))
    for i in range(1, 4):
        greet(zdev(i))
    greet(xdev(1))
    greet(xdev(-1))
    greet(sib)

    hf[...] = jnp.zeros_like(hf)
    x0[n, 0:128, :] = tok_in[...]
    x0[n, 128:144, :] = jnp.broadcast_to(gain_in[...].astype(F32), (16, 128)).astype(BF)
    for a in range(2):
        hf[:, 0:448] = up_q[a * 128:(a + 1) * 128, :].astype(F32) * up_s[...].astype(F32)[a:a + 1, :]
        for b in range(4):
            rows = 128 if b < 3 else 64
            block = hf[:, b * 128:(b + 1) * 128].T
            up[l, b * 128:b * 128 + rows, a * 128:(a + 1) * 128] = block[0:rows, :].astype(BF)
        block = dn_q[:, a * 128:(a + 1) * 128].astype(F32) * dn_s[...].astype(F32)[:, a:a + 1]
        dn[l, :, a * 128:(a + 1) * 128] = block.astype(BF)
    cot[n] = cot_in[...]
    pre[...] = jnp.zeros_like(pre)
    slope[...] = jnp.zeros_like(slope)

    @pl.when(moved)
    def _():
        pl.semaphore_wait(barrier, 18)

    @pl.when(jnp.logical_not(moved))
    def _():
        pl.semaphore_wait(barrier, 17)

    lg_up.z(1)
    lg_up.full(0)
    ag_x0.start()
    lg_up.z(2)
    lg_dn.full(0)
    sg_cot.scatter(cot_in)
    ag_x0.mid()
    lg_up.relay(0)
    lg_up.wait_z(1)
    lg_up.full(1)
    lg_up.z(3)
    lg_dn.relay(0)
    lg_up.wait_z(2)
    lg_up.full(2)
    lg_dn.z(1)
    ag_x0.end()
    ag_cot.start()
    normalize(x0)
    lg_up.done(0)
    pre_item(0)
    lg_up.relay(1)
    lg_up.wait_z(3)
    lg_up.full(3)
    lg_dn.z(2)
    lg_up.relay(2)
    ag_cot.mid()
    lg_dn.wait_z(1)
    lg_dn.full(1)
    lg_dn.z(3)
    lg_up.done(1)
    pre_item(1)
    lg_up.relay(3)
    lg_dn.wait_z(2)
    lg_dn.full(2)
    lg_up.done(2)
    pre_item(2)
    lg_dn.relay(1)
    lg_dn.wait_z(3)
    lg_dn.full(3)
    lg_up.done(3)
    pre_item(3)
    activate(h1t)
    lg_dn.done(0)
    out_item(hid, dn, 0, rs_1)
    sg_cot.seeded(cot_in)
    sg_cot.spread()
    lg_dn.relay(2)
    rs_1.combine(0)
    rs_1.spread(0, 0)
    rs_1.spread(1, 0)
    lg_dn.done(1)
    out_item(hid, dn, 1, rs_1)
    lg_dn.relay(3)
    rs_1.combine(1)
    rs_1.spread(0, 1)
    rs_1.spread(1, 1)
    lg_dn.done(2)
    out_item(hid, dn, 2, rs_1)
    rs_1.combine(2)
    rs_1.spread(0, 2)
    rs_1.spread(1, 2)
    lg_dn.done(3)
    out_item(hid, dn, 3, rs_1)
    rs_1.combine(3)
    rs_1.spread(0, 3)
    rs_1.spread(1, 3)
    ag_cot.end(slope_chunk)
    rs_1.cross()
    sg_cot.end(lambda q: None)
    rs_1.arrive(1)
    x1[n] = (x0[n, 0:128, :].astype(F32) + rs_1.finish()).astype(BF)

    ag_x1.start()
    pre[...] = jnp.zeros_like(pre)
    fac[...] = jnp.zeros_like(fac)
    ag_x1.mid()
    for i in range(1, 4):
        lg_h1.z(i)
    lg_h1.full(0)
    ag_x1.end(raw_chunk)
    factor = factor_of(fac[...])
    fac[...] = jnp.broadcast_to(factor, (128, 128))
    pre[...] = pre[...] * factor
    activate(h2t)
    for i in range(1, 4):
        lg_h1.wait_z(i)
        lg_h1.full(i)
    for i in range(1, 4):
        lg_h2.z(i)

    v = pre[...]
    sig = jax.nn.sigmoid(v)
    grad_pre = (slope[...] * (sig * (1.0 + v * (1.0 - sig)))).astype(BF)
    pulled = jnp.sum(grad_pre.astype(F32) * v, axis=1, keepdims=True)
    pulled = jnp.broadcast_to(pulled, (128, 128)).T[0:16, :].astype(BF)

    def put(j):
        pog[j, 128:144, :] = pulled
        psg[j, 128:144, :] = pulled

    loop(16, put)
    for i in range(4):
        loop(4, lambda q: out_chunk(grad_pre, up, flip(zl, i) * 4 + q, rs_g), unroll=True)
        rs_g.send(i)
        if i > 0:
            rs_g.combine(i - 1)
            rs_g.spread(0, i - 1)
    rs_g.combine(3)
    rs_g.spread(0, 3)
    for i in range(4):
        rs_g.spread(1, i)
    for i in range(4):
        out_item(hid, dn, i, rs_2)
    for i in range(4):
        rs_2.combine(i)
    rs_g.cross()
    for i in range(4):
        lg_h1.relay(i)
    rs_g.arrive(1)
    for i in range(4):
        rs_2.spread(0, i)
    for i in range(4):
        rs_2.spread(1, i)
    tot[...] = rs_g.finish()
    inner = jnp.broadcast_to(tot[128:129, :], (128, 128)).T / 4096.0
    x1_own = x1[n].astype(F32)
    scaled = tot[0:128, :] * gain_row(n)
    factor = fac[...]
    gp[...] = (cot[n].astype(F32) + factor * scaled - x1_own * factor * factor * inner).astype(BF)
    sg_g1.scatter(gp)
    lg_h2.full(0)
    for i in range(1, 4):
        lg_h2.wait_z(i)
        lg_h2.full(i)
    for i in range(4):
        lg_h1.done(i)
    gacc[...] = jnp.zeros_like(gacc)
    rs_2.cross()
    sg_g1.seeded(gp)
    sg_g1.spread()
    rs_2.arrive(1)

    def grad_chunk(hidden, grads):
        def one(q):
            right = jnp.concatenate([grads[q * 2], grads[q * 2 + 1]], axis=1)
            gacc[...] += lax.dot_general(hidden[q], right, NN, preferred_element_type=F32)
        return one

    for i in range(4):
        lg_h2.relay(i)
    states_out[...] = (x1_own + rs_2.finish()).astype(BF)
    for i in range(4):
        lg_h2.done(i)
        loop(4, lambda q: grad_chunk(h2t, cott)(flip(zl, i) * 4 + q), unroll=True)
    last = grad_chunk(h1t, g1t)
    sg_g1.end(lambda q: None)
    loop(16, last, unroll=4)
    grad_out[...] = gacc[...].astype(BF)
    sg_cot.scattered(cot_in)
    sg_g1.scattered(gp)
    drain()


def per_device(tokens, cotangent, gain, up_q, up_scale, down_q, down_scale):
    vmem = pl.BlockSpec(memory_space=pltpu.VMEM)

    def reduce_scratch(rows):
        wide = pltpu.VMEM((16, rows, 128), BF)
        one = pltpu.VMEM((rows, 128), BF)
        return [wide, wide, wide, pltpu.VMEM((2, 8, rows, 128), BF), one, one]

    full = pltpu.VMEM((16, 448, 256), BF)
    act = pltpu.VMEM((32, 128, 128), BF)
    hidden_all = pltpu.VMEM((16, 448, 128), BF)
    scratch = [
        full, full, pltpu.VMEM((32, 144, 128), BF), act, act, act, act,
        pltpu.VMEM((16, 128, 256), BF), hidden_all, hidden_all,
        pltpu.VMEM((128, 448), BF), pltpu.VMEM((128, 512), F32),
        pltpu.VMEM((128, 448), F32), pltpu.VMEM((128, 448), F32),
        pltpu.VMEM((448, 256), F32), pltpu.VMEM((128, 128), F32),
        pltpu.VMEM((128, 128), BF), pltpu.VMEM((144, 128), F32),
    ]
    scratch += reduce_scratch(128) + reduce_scratch(144) + reduce_scratch(128)
    scratch += [pltpu.SemaphoreType.DMA((N_SEND,)), pltpu.SemaphoreType.DMA((N_RECV,))]
    return pl.pallas_call(
        kernel,
        out_shape=(
            jax.ShapeDtypeStruct((128, 128), BF),
            jax.ShapeDtypeStruct((448, 256), BF),
        ),
        in_specs=[vmem] * 7,
        out_specs=(vmem, vmem),
        scratch_shapes=scratch,
        compiler_params=pltpu.CompilerParams(
            collective_id=0, has_side_effects=True, vmem_limit_bytes=48 << 20
        ),
        name="looped_block",
    )(tokens, cotangent, gain, up_q, up_scale, down_q, down_scale)


def solution(mesh):
    in_specs = (
        P("local", "node"),
        P("local", "node"),
        P(None, "node"),
        P("local", "node"),
        P("local", "node"),
        P("node", "local"),
        P("node", "local"),
    )
    out_specs = (P("local", "node"), P("node", "local"))
    return jax.shard_map(
        per_device, mesh=mesh, in_specs=in_specs, out_specs=out_specs, check_vma=False
    )
```

time: 197 us -> 178 us (0.904)
  the two profiles are of different devices: /device:TPU:27 before, /device:TPU:1 now
where the time goes in v2:
time: 178 us; the launch traced here: 177 us
  Pallas kernels  173 us (97%)
  local copies, waits for them, and re-layouts  3.34 us (2%)
    pallas_call x1, Pallas kernels, per_device(): pl.pallas_call(kernel, out_shape=(jax.ShapeDtypeStruct((128, 128), BF), j...  173 us

profile of v2, /device:TPU:1, one launch (start us, length us, event | category | flops | bytes accessed | tf_op | source)
XLA Modules:
  0.0 177.4 jit_solution(15363681947544297565)
XLA Ops:
  0.6 0.9 copy.10.dn_s
  1.5 0.0 copy-start
  1.5 0.0 copy-start.1
  1.5 0.0 copy-start.2
  1.5 0.0 copy-start.3
  1.5 0.0 copy-start.4
  1.5 1.1 copy.9.up_q
  2.7 0.0 copy-done
  2.7 0.0 copy-done.1
  2.7 0.0 copy-done.2
  2.7 0.0 copy-done.3
  2.7 0.0 copy-done.4
  2.7 173.3 %looped_block.1 = (bf16[128,128]{1,0:T(8,128)(2,1)S(1)}, bf16[448,256]{1,0:T(8,128)(2,1)S(1)}) custom-call(bf16[128,128]{1,0:T(8,128)(2,1)S(1)} %copy-done.1, bf16[128,128]{1,0:T(8,128)(2,1)S(1)} %copy-done.2, bf16[1,128]{1,0:T(2,128)(2,1)S(1)} %copy-done.4, bf16[256,448]{1,0:T(8,128)(2,1)S(1)} %copy.9.up_q, bf16[2,448]{1,0:T(2,128)(2,1)S(1)} %copy-done.3, ...), custom_call_target="tpu_custom_call" | custom-call | tf_op jit(solution)/shard_map/looped_block/pallas_call | solution.py:622
  176.1 0.6 copy.13
  176.7 0.7 copy.14
Async XLA Ops:
  1.5 1.2 copy-start
  1.5 1.2 copy-start.1
  1.5 1.2 copy-start.2
  1.5 1.2 copy-start.3
  1.5 1.2 copy-start.4

commit v3 on v2

--- a/solution.py
+++ b/solution.py
@@ -214,7 +214,7 @@
             from_y = (y - self.step(r, k) + 8) % 8
             return node_of((from_y + 4 * (k // 2)) % 8, (zh + k % 2) % 2, c)
 
-        def end(self, use):
+        def end(self, use, between=lambda: None):
             def move(r, k):
                 slot = self.arrival(r, k)
                 self.copy(slot, r * 4 + k, sib).wait_recv()
@@ -231,6 +231,8 @@
 
             loop(4, seeds)
             for r in range(3):
+                if r == 2:
+                    between()
                 loop(4, lambda k: move(r, k))
                 if r > 0:
                     loop(4, lambda k: finish(r - 1, k))
@@ -279,13 +281,10 @@
 
         def combine(self, i):
             got((self, "sib", i))
-            first = flip(zl, i) * 4
-
-            def add(q):
-                s = first + q
-                self.po[s] = (self.po[s].astype(F32) + self.r1[s].astype(F32)).astype(BF)
-
-            loop(4, add, unroll=True)
+            loop(4, lambda q: self.add_chunk(flip(zl, i) * 4 + q), unroll=True)
+
+        def add_chunk(self, q):
+            self.po[q] = (self.po[q].astype(F32) + self.r1[q].astype(F32)).astype(BF)
 
         def spread(self, kind, i):
             for q in range(2):
@@ -412,17 +411,18 @@
     greet(xdev(-1))
     greet(sib)
 
-    hf[...] = jnp.zeros_like(hf)
     x0[n, 0:128, :] = tok_in[...]
     x0[n, 128:144, :] = jnp.broadcast_to(gain_in[...].astype(F32), (16, 128)).astype(BF)
-    for a in range(2):
-        hf[:, 0:448] = up_q[a * 128:(a + 1) * 128, :].astype(F32) * up_s[...].astype(F32)[a:a + 1, :]
-        for b in range(4):
-            rows = 128 if b < 3 else 64
-            block = hf[:, b * 128:(b + 1) * 128].T
-            up[l, b * 128:b * 128 + rows, a * 128:(a + 1) * 128] = block[0:rows, :].astype(BF)
-        block = dn_q[:, a * 128:(a + 1) * 128].astype(F32) * dn_s[...].astype(F32)[:, a:a + 1]
-        dn[l, :, a * 128:(a + 1) * 128] = block.astype(BF)
+    for q_in, s_in, weight in ((up_q, up_s, up), (dn_q, dn_s, dn)):
+        for a in range(2):
+            cols = pl.ds(a * 128, 128)
+            for b in range(4):
+                size = 128 if b < 3 else 64
+                rows = pl.ds(b * 128, size)
+                hf[0:128, 0:size] = jnp.broadcast_to(s_in[a:a + 1, rows].astype(F32), (128, size))
+                scale = hf[:, 0:128].T[0:size, :]
+                weight[l, rows, cols] = (q_in[rows, cols].astype(F32) * scale).astype(BF)
+    hf[...] = jnp.zeros_like(hf)
     cot[n] = cot_in[...]
     pre[...] = jnp.zeros_like(pre)
     slope[...] = jnp.zeros_like(slope)
@@ -482,6 +482,7 @@
     sg_cot.seeded(cot_in)
     sg_cot.spread()
     lg_dn.relay(2)
+    ag_cot.end()
     rs_1.combine(0)
     rs_1.spread(0, 0)
     rs_1.spread(1, 0)
@@ -501,15 +502,15 @@
     rs_1.combine(3)
     rs_1.spread(0, 3)
     rs_1.spread(1, 3)
-    ag_cot.end(slope_chunk)
+    loop(16, slope_chunk, unroll=4)
     rs_1.cross()
-    sg_cot.end(lambda q: None)
     rs_1.arrive(1)
     x1[n] = (x0[n, 0:128, :].astype(F32) + rs_1.finish()).astype(BF)
 
     ag_x1.start()
     pre[...] = jnp.zeros_like(pre)
     fac[...] = jnp.zeros_like(fac)
+    sg_cot.end(lambda q: None)
     ag_x1.mid()
     for i in range(1, 4):
         lg_h1.z(i)
@@ -553,11 +554,11 @@
     rs_g.cross()
     for i in range(4):
         lg_h1.relay(i)
+    lg_h2.full(0)
+    for i in range(1, 4):
+        lg_h2.wait_z(i)
+        lg_h2.full(i)
     rs_g.arrive(1)
-    for i in range(4):
-        rs_2.spread(0, i)
-    for i in range(4):
-        rs_2.spread(1, i)
     tot[...] = rs_g.finish()
     inner = jnp.broadcast_to(tot[128:129, :], (128, 128)).T / 4096.0
     x1_own = x1[n].astype(F32)
@@ -565,17 +566,16 @@
     factor = fac[...]
     gp[...] = (cot[n].astype(F32) + factor * scaled - x1_own * factor * factor * inner).astype(BF)
     sg_g1.scatter(gp)
-    lg_h2.full(0)
-    for i in range(1, 4):
-        lg_h2.wait_z(i)
-        lg_h2.full(i)
+    for i in range(4):
+        rs_2.spread(0, i)
+    for i in range(4):
+        rs_2.spread(1, i)
     for i in range(4):
         lg_h1.done(i)
+        lg_h2.relay(i)
     gacc[...] = jnp.zeros_like(gacc)
-    rs_2.cross()
     sg_g1.seeded(gp)
     sg_g1.spread()
-    rs_2.arrive(1)
 
     def grad_chunk(hidden, grads):
         def one(q):
@@ -584,14 +584,12 @@
         return one
 
     for i in range(4):
-        lg_h2.relay(i)
-    states_out[...] = (x1_own + rs_2.finish()).astype(BF)
-    for i in range(4):
         lg_h2.done(i)
         loop(4, lambda q: grad_chunk(h2t, cott)(flip(zl, i) * 4 + q), unroll=True)
     last = grad_chunk(h1t, g1t)
-    sg_g1.end(lambda q: None)
-    loop(16, last, unroll=4)
+    sg_g1.end(last, rs_2.cross)
+    rs_2.arrive(1)
+    states_out[...] = (x1_own + rs_2.finish()).astype(BF)
     grad_out[...] = gacc[...].astype(BF)
     sg_cot.scattered(cot_in)
     sg_g1.scattered(gp)
@@ -632,7 +630,7 @@
             collective_id=0, has_side_effects=True, vmem_limit_bytes=48 << 20
         ),
         name="looped_block",
-    )(tokens, cotangent, gain, up_q, up_scale, down_q, down_scale)
+    )(tokens, cotangent, gain, up_q.T, up_scale, down_q, down_scale.T)
 
 
 def solution(mesh):

time: 178 us -> 176 us (0.989)
  Pallas kernels: 173 us -> 169 us
  local copies, waits for them, and re-layouts: 3.34 us -> 6.05 us
    pallas_call x1, Pallas kernels: 173 us -> 169 us  [per_device(): pl.pallas_call(kernel, out_shape=(jax.ShapeDtypeStruct((128, 128), BF), j...]
    unnamed x14 -> x16, local copies, waits for them, and re-layouts: 3.34 us -> 6.05 us
where the time goes in v3:
time: 176 us
  Pallas kernels  169 us (96%)
  local copies, waits for them, and re-layouts  6.05 us (3%)
    pallas_call x1, Pallas kernels, per_device(): pl.pallas_call(kernel, out_shape=(jax.ShapeDtypeStruct((128, 128), BF), j...  169 us
    unnamed x16, local copies, waits for them, and re-layouts  6.05 us

profile of v3, /device:TPU:1, one launch (start us, length us, event | category | flops | bytes accessed | tf_op | source)
XLA Modules:
  0.0 175.6 jit_solution(605468692656168467)
XLA Ops:
  0.6 0.0 copy-start.4
  0.6 0.0 copy-start.6
  0.7 0.7 copy-done.4
  1.3 0.0 copy-done.6
  1.3 0.0 copy-start
  1.3 0.9 copy-done
  2.3 0.0 copy-start.1
  2.3 0.9 copy-done.1
  3.2 0.0 copy-start.2
  3.2 0.8 copy-done.2
  4.0 0.0 copy-start.3
  4.0 0.8 copy-done.3
  4.7 0.0 copy-start.5
  4.7 0.7 copy-done.5
  5.4 168.9 %looped_block.1 = (bf16[128,128]{1,0:T(8,128)(2,1)S(1)}, bf16[448,256]{1,0:T(8,128)(2,1)S(1)}) custom-call(bf16[128,128]{1,0:T(8,128)(2,1)S(1)} %copy-done.2, bf16[128,128]{1,0:T(8,128)(2,1)S(1)} %copy-done.3, bf16[1,128]{1,0:T(2,128)(2,1)S(1)} %copy-done.6, bf16[448,256]{1,0:T(8,128)(2,1)S(1)} %bitcast.2, bf16[2,448]{1,0:T(2,128)(2,1)S(1)} %copy-done.4, ...), custom_call_target="tpu_custom_call" | custom-call | tf_op jit(solution)/shard_map/looped_block/pallas_call | solution.py:620
  174.3 0.6 copy.11
  174.9 0.7 copy.12
Async XLA Ops:
  0.6 0.7 copy-start.4
  0.6 0.7 copy-start.6
  1.3 0.9 copy-start
  2.3 0.9 copy-start.1
  3.2 0.8 copy-start.2
  4.0 0.8 copy-start.3
  4.7 0.7 copy-start.5

commit v4 on v3

--- a/solution.py
+++ b/solution.py
@@ -118,10 +118,12 @@
         def from_y(self, j, zh_):
             return node_of((y - peer(j) + 8) % 8, zh_, c)
 
+        def first(self):
+            go((self, "zh"), 1, lambda j: self.copy(n, 1, zhp))
+            go((self, "sib"), 1, lambda j: self.copy(n, 0, sib))
+
         def start(self):
-            go((self, "zh"), 1, lambda j: self.copy(n, 1, zhp))
             go((self, "own"), 7, lambda j: self.copy(n, 2 + j, ydev(peer(j))))
-            go((self, "sib"), 1, lambda j: self.copy(n, 0, sib))
 
         def mid(self):
             got((self, "zh"))
@@ -294,6 +296,14 @@
                 @pl.when(to != y)
                 def _():
                     rc(src, self.r2.at[kind, y], self.left, self.base + 4 + kind, (node_of(to, zh, c), l)).start()
+
+        def spread_all(self, kind):
+            def one(j):
+                to = (y + peer(j)) % 8
+                src = self.po.at[to * 2 + (1 - zh if kind == 0 else zh)]
+                rc(src, self.r2.at[kind, y], self.left, self.base + 4 + kind, ydev(peer(j))).start()
+
+            loop(7, one)
 
         def arrive(self, kind):
             view = self.r2.at[kind, pl.ds(0, 7)]
@@ -435,6 +445,8 @@
     def _():
         pl.semaphore_wait(barrier, 17)
 
+    ag_x0.first()
+    ag_cot.first()
     lg_up.z(1)
     lg_up.full(0)
     ag_x0.start()
@@ -453,6 +465,7 @@
     ag_x0.end()
     ag_cot.start()
     normalize(x0)
+    ag_cot.mid()
     lg_up.done(0)
     pre_item(0)
     lg_up.relay(1)
@@ -460,7 +473,6 @@
     lg_up.full(3)
     lg_dn.z(2)
     lg_up.relay(2)
-    ag_cot.mid()
     lg_dn.wait_z(1)
     lg_dn.full(1)
     lg_dn.z(3)
@@ -507,6 +519,7 @@
     rs_1.arrive(1)
     x1[n] = (x0[n, 0:128, :].astype(F32) + rs_1.finish()).astype(BF)
 
+    ag_x1.first()
     ag_x1.start()
     pre[...] = jnp.zeros_like(pre)
     fac[...] = jnp.zeros_like(fac)
@@ -542,11 +555,9 @@
         rs_g.send(i)
         if i > 0:
             rs_g.combine(i - 1)
-            rs_g.spread(0, i - 1)
     rs_g.combine(3)
-    rs_g.spread(0, 3)
-    for i in range(4):
-        rs_g.spread(1, i)
+    rs_g.spread_all(0)
+    rs_g.spread_all(1)
     for i in range(4):
         out_item(hid, dn, i, rs_2)
     for i in range(4):
@@ -566,10 +577,8 @@
     factor = fac[...]
     gp[...] = (cot[n].astype(F32) + factor * scaled - x1_own * factor * factor * inner).astype(BF)
     sg_g1.scatter(gp)
-    for i in range(4):
-        rs_2.spread(0, i)
-    for i in range(4):
-        rs_2.spread(1, i)
+    rs_2.spread_all(0)
+    rs_2.spread_all(1)
     for i in range(4):
         lg_h1.done(i)
         lg_h2.relay(i)

time: 176 us -> 177 us (level)
  no operation moved by 1% of the time
where the time goes in v4:
time: 177 us; the launch traced here: 176 us
  Pallas kernels  170 us (96%)
  local copies, waits for them, and re-layouts  6.05 us (3%)
    pallas_call x1, Pallas kernels, per_device(): pl.pallas_call(kernel, out_shape=(jax.ShapeDtypeStruct((128, 128), BF), j...  170 us
    unnamed x16, local copies, waits for them, and re-layouts  6.05 us

profile of v4, /device:TPU:1, one launch (start us, length us, event | category | flops | bytes accessed | tf_op | source)
XLA Modules:
  0.0 176.4 jit_solution(764657878507733508)
XLA Ops:
  0.6 0.0 copy-start.4
  0.6 0.0 copy-start.6
  0.7 0.7 copy-done.4
  1.3 0.0 copy-done.6
  1.3 0.0 copy-start
  1.3 0.9 copy-done
  2.3 0.0 copy-start.1
  2.3 0.9 copy-done.1
  3.2 0.0 copy-start.2
  3.2 0.8 copy-done.2
  4.0 0.0 copy-start.3
  4.0 0.8 copy-done.3
  4.7 0.0 copy-start.5
  4.7 0.7 copy-done.5
  5.4 169.7 %looped_block.1 = (bf16[128,128]{1,0:T(8,128)(2,1)S(1)}, bf16[448,256]{1,0:T(8,128)(2,1)S(1)}) custom-call(bf16[128,128]{1,0:T(8,128)(2,1)S(1)} %copy-done.2, bf16[128,128]{1,0:T(8,128)(2,1)S(1)} %copy-done.3, bf16[1,128]{1,0:T(2,128)(2,1)S(1)} %copy-done.6, bf16[448,256]{1,0:T(8,128)(2,1)S(1)} %bitcast.2, bf16[2,448]{1,0:T(2,128)(2,1)S(1)} %copy-done.4, ...), custom_call_target="tpu_custom_call" | custom-call | tf_op jit(solution)/shard_map/looped_block/pallas_call | solution.py:629
  175.1 0.6 copy.11
  175.7 0.7 copy.12
Async XLA Ops:
  0.6 0.7 copy-start.4
  0.6 0.7 copy-start.6
  1.3 0.9 copy-start
  2.3 0.9 copy-start.1
  3.2 0.8 copy-start.2
  4.0 0.8 copy-start.3
  4.7 0.7 copy-start.5
